TPU v7x, 256 devices: a whole 4x4x8 slice. The times are simulated.
256 devices in a mesh: group: 4 (over z_lo, core), tile: 64 (over x, z_hi, y).
Axes of the slice: x: 4, y: 4, z: 8 (z_hi: 4, z_lo: 2; z = z_hi * 2 + z_lo), core: 2. Of those that a mesh axis runs over, the one named last changes fastest.
Arguments:
- object_slices: bfloat16 [4, 2048, 8192], P(None, 'group', 'tile'), may hold values from -4 to 4
- probe: float32 [1024, 256], replicated, may hold values from -6 to 6
- mid_waves: bfloat16 [4, 64, 3, 2, 2, 256, 256], P('group', 'tile'), may hold values from -160 to 160
- amplitudes: bfloat16 [4, 64, 3, 256, 256], P('group', 'tile'), may hold values from 0.19921875 to 4
- row_offsets: int32 [4, 64, 3], P('group', 'tile'), may hold values from 0 to 256
- col_offsets: int32 [4, 64, 3], P('group', 'tile'), may hold values from 0 to 128
Outputs:
- object_new: float32 [4, 2048, 8192], P(None, 'group', 'tile')
- probe_new: float32 [1024, 256], P('tile')
All inputs are finite; a program needn't handle non-finite values.
Results may differ from a plain program's by a relative error of at most 0.0003.
Values may be sent and summed in bfloat16 or wider, within the bound.
A program may use at most 128 MiB of HBM per device.

v0:
```python
import jax
import jax.numpy as jnp
from jax import lax
from jax.sharding import PartitionSpec as P

phase_rate = 0.25
floor_level = 0.5
object_step = 0.5
probe_step = 0.5
epsilon = 1e-06


def with_halo(cells, sides, width):
    for axis, dim in sides:
        count = lax.axis_size(axis)
        ends = count - 1
        head = lax.slice_in_dim(cells, 0, width, axis=dim)
        tail = lax.slice_in_dim(cells, cells.shape[dim] - width, cells.shape[dim], axis=dim)
        cells = jnp.concatenate(
            [
                lax.ppermute(tail, axis, [(i, (i + 1) % count) for i in range(ends)]),
                cells,
                lax.ppermute(head, axis, [((i + 1) % count, i) for i in range(ends)]),
            ],
            axis=dim,
        )
    return cells


def passed_along(block, axis, distance):
    devices = range(lax.axis_size(axis))
    route = [(i - distance, i) for i in devices if i - distance in devices]
    return lax.ppermute(block, axis, route)


def dft_tables(length):
    index = jnp.arange(length, dtype=jnp.int32)
    product = index[:, None] * index[None, :] % length
    angle = product.astype(jnp.float32) * (2.0 * jnp.pi / length)
    norming = 1.0 / jnp.sqrt(jnp.float32(length))
    return (jnp.cos(angle) * norming, jnp.sin(angle) * norming)


def back_tables(length):
    freq = jnp.arange(length, dtype=jnp.int32)
    freq = jnp.where(freq < length // 2, freq, freq - length).astype(jnp.float32)
    phase = (
        2.0
        * jnp.pi
        * phase_rate
        / length
        * (freq[:, None] * freq[:, None] + freq[None, :] * freq[None, :])
    )
    return (jnp.cos(phase), jnp.sin(phase))


def spectral(real_part, imag_part, cos_table, sin_table, direction):
    highest = lax.Precision.HIGHEST
    signed = sin_table * direction
    left_real = jnp.matmul(cos_table, real_part, precision=highest) - jnp.matmul(
        signed, imag_part, precision=highest
    )
    left_imag = jnp.matmul(cos_table, imag_part, precision=highest) + jnp.matmul(
        signed, real_part, precision=highest
    )
    out_real = jnp.matmul(left_real, cos_table, precision=highest) - jnp.matmul(
        left_imag, signed, precision=highest
    )
    out_imag = jnp.matmul(left_imag, cos_table, precision=highest) + jnp.matmul(
        left_real, signed, precision=highest
    )
    return (out_real, out_imag)


def shards(object_slices, probe, mid_waves, amplitudes, row_offsets, col_offsets):
    row_count = object_slices.shape[1]
    strip_width = object_slices.shape[2]
    probe_size = probe.shape[1]
    mode_count = probe.shape[0] // (2 * probe_size)
    padded = with_halo(object_slices, (("tile", 2),), strip_width).astype(jnp.float32)
    probe_parts = probe.reshape(2, mode_count, probe_size, probe_size)
    cos_table, sin_table = dft_tables(probe_size)
    kernel_real, kernel_imag = back_tables(probe_size)
    grad_obj = jnp.zeros(padded.shape, jnp.float32)
    grad_probe = jnp.zeros((2, mode_count, probe_size, probe_size), jnp.float32)
    anchor = jnp.zeros((), jnp.int32)
    for position in range(mid_waves.shape[2]):
        row_at = row_offsets[0, 0, position]
        col_at = col_offsets[0, 0, position]
        patch = lax.dynamic_slice(padded, (anchor, row_at, col_at), (4, probe_size, probe_size))
        first_real, first_imag, second_real, second_imag = (patch[0], patch[1], patch[2], patch[3])
        wave = mid_waves[0, 0, position].astype(jnp.float32)
        mid_real, mid_imag = (wave[0], wave[1])
        amp = amplitudes[0, 0, position].astype(jnp.float32)
        exit_real = mid_real * second_real - mid_imag * second_imag
        exit_imag = mid_real * second_imag + mid_imag * second_real
        far_real, far_imag = spectral(exit_real, exit_imag, cos_table, sin_table, -1.0)
        power = jnp.sum(far_real * far_real + far_imag * far_imag, axis=0)
        factor = 1.0 - amp / jnp.maximum(jnp.sqrt(power), floor_level)
        chi_real, chi_imag = spectral(
            far_real * factor, far_imag * factor, cos_table, sin_table, 1.0
        )
        second_grad_real = jnp.sum(mid_real * chi_real + mid_imag * chi_imag, axis=0)
        second_grad_imag = jnp.sum(mid_real * chi_imag - mid_imag * chi_real, axis=0)
        back_real = second_real * chi_real + second_imag * chi_imag
        back_imag = second_real * chi_imag - second_imag * chi_real
        spec_real, spec_imag = spectral(back_real, back_imag, cos_table, sin_table, -1.0)
        turned_real = spec_real * kernel_real - spec_imag * kernel_imag
        turned_imag = spec_real * kernel_imag + spec_imag * kernel_real
        wave_real, wave_imag = spectral(turned_real, turned_imag, cos_table, sin_table, 1.0)
        first_grad_real = jnp.sum(probe_parts[0] * wave_real + probe_parts[1] * wave_imag, axis=0)
        first_grad_imag = jnp.sum(probe_parts[0] * wave_imag - probe_parts[1] * wave_real, axis=0)
        probe_real = first_real * wave_real + first_imag * wave_imag
        probe_imag = first_real * wave_imag - first_imag * wave_real
        grad_probe = grad_probe + jnp.stack([probe_real, probe_imag])
        update = jnp.stack([first_grad_real, first_grad_imag, second_grad_real, second_grad_imag])
        previous = lax.dynamic_slice(
            grad_obj, (anchor, row_at, col_at), (4, probe_size, probe_size)
        )
        grad_obj = lax.dynamic_update_slice(grad_obj, previous + update, (anchor, row_at, col_at))
    left_rim = grad_obj[:, :, :strip_width]
    right_rim = grad_obj[:, :, 2 * strip_width :]
    own_grad = grad_obj[:, :, strip_width : 2 * strip_width]
    own_grad = own_grad + passed_along(left_rim, "tile", -1)
    own_grad = own_grad + passed_along(right_rim, "tile", 1)
    object_squares = jnp.sum(own_grad * own_grad)
    flat_probe = grad_probe.reshape(2 * mode_count * probe_size, probe_size)
    share = flat_probe.shape[0] // lax.axis_size("tile")
    start_row = lax.axis_index("tile") * share
    probe_total = lax.psum(flat_probe, ("group", "tile"))
    probe_shard = lax.dynamic_slice_in_dim(probe_total, start_row, share, 0)
    object_total = lax.psum(object_squares, ("group", "tile"))
    probe_squares = jnp.sum(probe_total * probe_total)
    object_count = 4 * row_count * strip_width * lax.axis_size("group") * lax.axis_size("tile")
    object_rms = jnp.sqrt(object_total / object_count + epsilon)
    object_new = padded[:, :, strip_width : 2 * strip_width] - object_step * own_grad / object_rms
    probe_count = 2 * mode_count * probe_size * probe_size
    probe_rms = jnp.sqrt(probe_squares / probe_count + epsilon)
    probe_rows = lax.dynamic_slice_in_dim(probe, start_row, share, 0)
    probe_new = probe_rows - probe_step * probe_shard / probe_rms
    return (object_new, probe_new)


def solution(mesh):
    return jax.shard_map(
        shards,
        mesh=mesh,
        in_specs=(
            P(None, "group", "tile"),
            P(),
            P("group", "tile", None, None, None, None, None),
            P("group", "tile", None, None, None),
            P("group", "tile", None),
            P("group", "tile", None),
        ),
        out_specs=(P(None, "group", "tile"), P("tile", None)),
        check_vma=False,
    )
```

profile of v0, /device:TPU:1, one launch (start us, length us, event | category | flops | bytes accessed | tf_op | source)
XLA Modules:
  0.0 642.6 jit_solution(9129326133849237512)
XLA Ops:
  7.2 5.0 collective-permute-start
  36.2 1.7 fusion.182
  37.9 1.7 fusion.186
  39.6 1.7 fusion.152
  41.3 2.0 fusion.156
  43.4 1.7 fusion.6
  45.1 1.7 fusion.7
  51.5 1.7 fusion.22
  53.2 1.7 fusion.23
  54.9 1.7 fusion.184
  66.3 1.8 convolution_subtract_fusion.14
  78.2 2.1 fusion.13
  85.0 2.4 add_reduce_fusion.3
  90.7 1.9 fusion.11
  100.6 1.7 fusion.134
  102.3 1.7 fusion.130
  104.0 1.9 fusion.42
  115.6 2.1 add_reduce_fusion.6
  117.6 1.7 fusion.172
  121.0 1.7 fusion.19
  124.3 1.7 fusion.18
  129.2 1.7 convolution_add_fusion.18
  130.9 1.7 fusion.164
  141.0 1.8 fusion.117
  145.9 2.4 add_reduce_fusion
  150.0 1.7 fusion.108
  151.7 1.7 fusion.3
  153.4 2.0 fusion.110
  155.4 1.7 fusion.2
  165.3 1.7 fusion.9
  167.0 1.7 fusion.132
  168.7 1.7 fusion.8
  176.8 1.7 fusion.16
  178.5 1.8 fusion.158
  186.7 1.7 fusion
  190.0 1.8 convolution_subtract_fusion
  193.4 5.2 add_bitcast_fusion
  199.8 16.8 %dynamic_update_slice.9 = f32[4,512,384]{2,1,0:T(8,128)S(1)} dynamic-update-slice(f32[4,512,384]{2,1,0:T(8,128)S(1)} %broadcast_in_dim.2, f32[4,256,256]{2,1,0:T(8,128)} %pad_maximum_fusion, s32[]{:T(128)} %constant.21.clone.1, s32[]{:T(128)S(6)} %select_n.264, s32[]{:T(128)S(6)} %select_n.265) | dynamic-update-slice | bytes 2097156 | tf_op jit(solution)/shard_map/dynamic_update_slice | solution.py:120
  216.6 2.5 maximum_add_fusion
  219.1 15.5 %dynamic_update_slice.10 = f32[4,512,384]{2,1,0:T(8,128)S(1)} dynamic-update-slice(f32[4,512,384]{2,1,0:T(8,128)S(1)} %dynamic_update_slice.9, f32[4,256,256]{2,1,0:T(8,128)} %maximum_add_fusion, s32[]{:T(128)} %constant.21.clone.1, s32[]{:T(128)S(6)} %select_n.267, s32[]{:T(128)S(6)} %select_n.268) | dynamic-update-slice | bytes 2097156 | tf_op jit(solution)/shard_map/dynamic_update_slice | solution.py:120
  234.6 2.5 maximum_add_fusion.1
  237.1 15.6 %dynamic_update_slice.11 = f32[4,512,384]{2,1,0:T(8,128)S(1)} dynamic-update-slice(f32[4,512,384]{2,1,0:T(8,128)S(1)} %dynamic_update_slice.10, f32[4,256,256]{2,1,0:T(8,128)} %maximum_add_fusion.1, s32[]{:T(128)} %constant.21.clone.1, s32[]{:T(128)S(6)} %select_n.269, s32[]{:T(128)S(6)} %select_n.270) | dynamic-update-slice | bytes 2097156 | tf_op jit(solution)/shard_map/dynamic_update_slice | solution.py:120
  255.7 5.0 collective-permute-start.3
  261.9 285.6 %all-reduce.2.cloned.1.call-done = f32[1024,256]{1,0:T(8,128)} async-done(((f32[1024,256]{1,0:T(8,128)}), f32[1024,256]{1,0:T(8,128)}) %all-reduce.2.cloned.1.call-update) | async-done | bytes 1048592 | tf_op jit(solution)/shard_map/psum | solution.py:130
  547.5 2.1 multiply_reduce_fusion
  550.3 2.4 multiply_reduce_fusion.1
  554.1 77.5 %psum.14 = f32[]{:T(128)} all-reduce(f32[]{:T(128)} %multiply_reduce_fusion.1), channel_id=1, replica_groups=mesh['group'=4,'tile'=64] {'group','tile'}, use_global_device_ids=true, to_apply=%region_16.17 | all-reduce | flops 1 | bytes 8 | tf_op jit(solution)/shard_map/psum | solution.py:132
  632.3 3.0 slice_subtract_fusion
  (102 shorter events, 112.7 us)
Async XLA Ops:
  7.2 23.0 %copy-start.7 = (bf16[1,1,3,2,2,256,256]{6,5,4,3,2,1,0:T(8,128)(2,1)S(1)}, bf16[1,1,3,2,2,256,256]{6,5,4,3,2,1,0:T(8,128)(2,1)}, u32[]{:S(2)}) copy-start(bf16[1,1,3,2,2,256,256]{6,5,4,3,2,1,0:T(8,128)(2,1)} %param.8) | copy-start | bytes 4718596
  7.2 540.3 %all-reduce.2.cloned.1.call-start = ((), (), s32[]{:S(2)}) async-start(), calls=%async_computation | async-start | bytes 2097152 | tf_op jit(solution)/shard_map/psum | solution.py:130
  7.2 23.2 %collective-permute-start = (bf16[4,512,128]{2,1,0:T(8,128)(2,1)}, bf16[4,512,128]{2,1,0:T(8,128)(2,1)}, u32[]{:S(2)}, u32[]{:S(2)}) collective-permute-start(bf16[4,512,128]{2,1,0:T(8,128)(2,1)} %param.6), channel_id=1, source_target_pairs={{0,1},{1,2},{2,3},{3,4},{4,5},{5,6},{6,7},{7,8},{8,9},{9,10},{10,1... | collective-permute-start | bytes 1572872 | tf_op jit(solution)/shard_map/ppermute | solution.py:21
  12.2 18.3 %collective-permute-start.1 = (bf16[4,512,128]{2,1,0:T(8,128)(2,1)}, bf16[4,512,128]{2,1,0:T(8,128)(2,1)}, u32[]{:S(2)}, u32[]{:S(2)}) collective-permute-start(bf16[4,512,128]{2,1,0:T(8,128)(2,1)} %param.6), channel_id=1, source_target_pairs={{1,0},{2,1},{3,2},{4,3},{5,4},{6,5},{7,6},{8,7},{9,8},{10,9},{11,1... | collective-permute-start | bytes 1572872 | tf_op jit(solution)/shard_map/ppermute | solution.py:23
  25.3 5.2 copy-start.8
  31.9 13.2 %copy-start = (f32[4,512,384]{2,1,0:T(8,128)}, f32[4,512,384]{2,1,0:T(8,128)S(1)}, u32[]{:S(2)}) copy-start(f32[4,512,384]{2,1,0:T(8,128)S(1)} %maximum_convert_fusion) | copy-start | bytes 9437188
  68.1 4.8 copy-start.9
  252.7 8.0 %copy-start.1 = (f32[1,2,256,256]{3,2,1,0:T(8,128)S(1)}, f32[1,2,256,256]{3,2,1,0:T(8,128)}, u32[]{:S(2)}) copy-start(f32[1,2,256,256]{3,2,1,0:T(8,128)} %get-tuple-element.32) | copy-start | bytes 1572868
  252.7 8.0 %copy-start.2 = (f32[1,2,256,256]{3,2,1,0:T(8,128)S(1)}, f32[1,2,256,256]{3,2,1,0:T(8,128)}, u32[]{:S(2)}) copy-start(f32[1,2,256,256]{3,2,1,0:T(8,128)} %get-tuple-element.33) | copy-start | bytes 1572868
  252.7 8.0 %copy-start.3 = (f32[1,2,256,256]{3,2,1,0:T(8,128)S(1)}, f32[1,2,256,256]{3,2,1,0:T(8,128)}, u32[]{:S(2)}) copy-start(f32[1,2,256,256]{3,2,1,0:T(8,128)} %get-tuple-element.47) | copy-start | bytes 1572868
  252.7 8.0 %copy-start.4 = (f32[1,2,256,256]{3,2,1,0:T(8,128)S(1)}, f32[1,2,256,256]{3,2,1,0:T(8,128)}, u32[]{:S(2)}) copy-start(f32[1,2,256,256]{3,2,1,0:T(8,128)} %get-tuple-element.48) | copy-start | bytes 1572868
  252.8 7.9 %copy-start.5 = (f32[1,2,256,256]{3,2,1,0:T(8,128)S(1)}, f32[1,2,256,256]{3,2,1,0:T(8,128)}, u32[]{:S(2)}) copy-start(f32[1,2,256,256]{3,2,1,0:T(8,128)} %get-tuple-element.49) | copy-start | bytes 1572868
  252.8 7.9 %copy-start.6 = (f32[1,2,256,256]{3,2,1,0:T(8,128)S(1)}, f32[1,2,256,256]{3,2,1,0:T(8,128)}, u32[]{:S(2)}) copy-start(f32[1,2,256,256]{3,2,1,0:T(8,128)} %get-tuple-element.50) | copy-start | bytes 1572868
  254.3 296.0 %collective-permute-start.2 = (f32[4,512,128]{2,1,0:T(8,128)}, f32[4,512,128]{2,1,0:T(8,128)}, u32[]{:S(2)}, u32[]{:S(2)}) collective-permute-start(f32[4,512,128]{2,1,0:T(8,128)} %get-tuple-element.30), channel_id=1, source_target_pairs={{1,0},{2,1},{3,2},{4,3},{5,4},{6,5},{7,6},{8,7},{9,8},{10,9},{11,1... | collective-permute-start | bytes 3145736 | tf_op jit(solution)/shard_map/ppermute | solution.py:33
  255.7 294.6 %collective-permute-start.3 = (f32[4,512,128]{2,1,0:T(8,128)}, f32[4,512,128]{2,1,0:T(8,128)}, u32[]{:S(2)}, u32[]{:S(2)}) collective-permute-start(f32[4,512,128]{2,1,0:T(8,128)} %get-tuple-element.31), channel_id=1, source_target_pairs={{0,1},{1,2},{2,3},{3,4},{4,5},{5,6},{6,7},{7,8},{8,9},{9,10},{10,1... | collective-permute-start | bytes 3145736 | tf_op jit(solution)/shard_map/ppermute | solution.py:33
Sparse Core Ops, SparseCore 0:
  262.0 285.3 all-reduce.1
where the time goes:
time: 653 us; the launch traced here: 643 us
  waiting for transfers between devices  286 us (44%)
  matrix products  165 us (25%)
  blocking collectives  77.5 us (12%)
  local copies, waits for them, and re-layouts  54.7 us (8%)
  between operations  28.3 us (4%)
  other arithmetic  19.1 us (3%)
  starting transfers between devices  12.7 us (2%)
    psum x1, waiting for transfers between devices, shards(): probe_total = lax.psum(flat_probe, ('group', 'tile'))  286 us
    psum x1, blocking collectives, shards(): object_total = lax.psum(object_squares, ('group', 'tile'))  77.5 us
    dynamic_update_slice x3, local copies, waits for them, and re-layouts, shards(): lax.dynamic_update_slice(grad_obj, previous + update, (anchor, row_at, co...  47.9 us
    dot_general x12, matrix products, spectral(): jnp.matmul(left_imag, signed, precision=highest)  22.9 us
    dot_general x12, matrix products, spectral(): jnp.matmul(left_real, signed, precision=highest)  21.2 us
    dot_general x12, matrix products, spectral(): jnp.matmul(signed, imag_part, precision=highest)  20.8 us
    dot_general x12, matrix products, spectral(): jnp.matmul(cos_table, real_part, precision=highest)  20.7 us
    dot_general x12, matrix products, spectral(): jnp.matmul(signed, real_part, precision=highest)  20.2 us
  transfers between devices with their start and end apart: 5, of which 1 were waited for; matrix products, arithmetic and copies ran while one was open for 1% of the time, Pallas kernels for 0%

commit v1 on v0

--- a/solution.py
+++ b/solution.py
@@ -127,7 +127,15 @@
     flat_probe = grad_probe.reshape(2 * mode_count * probe_size, probe_size)
     share = flat_probe.shape[0] // lax.axis_size("tile")
     start_row = lax.axis_index("tile") * share
-    probe_total = lax.psum(flat_probe, ("group", "tile"))
+
+    def heads_state(x_in):
+        chip_axis = "tile"
+        axis_id = "group"
+        for j0 in (axis_id, chip_axis):
+            x_in = lax.psum(x_in, axis_name=j0)
+        return x_in
+
+    probe_total = heads_state(flat_probe)
     probe_shard = lax.dynamic_slice_in_dim(probe_total, start_row, share, 0)
     object_total = lax.psum(object_squares, ("group", "tile"))
     probe_squares = jnp.sum(probe_total * probe_total)

time: 653 us -> 1040 us (1.59)
  the two profiles are of different devices: /device:TPU:1 before, /device:TPU:8 now
where the time goes in v1:
time: 1040 us; the launch traced here: 1030 us
  waiting for transfers between devices  639 us (61%)
  matrix products  163 us (16%)
  blocking collectives  114 us (11%)
  local copies, waits for them, and re-layouts  50.5 us (5%)
  between operations  28.3 us (3%)
  other arithmetic  19.2 us (2%)
  starting transfers between devices  13.7 us (1%)
    psum x2, waiting for transfers between devices, heads_state(): x_in = lax.psum(x_in, axis_name=j0)  615 us
    psum x1, blocking collectives, shards(): object_total = lax.psum(object_squares, ('group', 'tile'))  114 us
    dynamic_update_slice x3, local copies, waits for them, and re-layouts, shards(): lax.dynamic_update_slice(grad_obj, previous + update, (anchor, row_at, co...  43 us
    ppermute x2, waiting for transfers between devices, passed_along(): return lax.ppermute(block, axis, route)  23.9 us
    dot_general x12, matrix products, spectral(): jnp.matmul(left_real, signed, precision=highest)  21.2 us
    dot_general x12, matrix products, spectral(): jnp.matmul(left_imag, signed, precision=highest)  21.1 us
  transfers between devices with their start and end apart: 6, of which 4 were waited for; matrix products, arithmetic and copies ran while one was open for 6% of the time, Pallas kernels for 0%

profile of v1, /device:TPU:8, one launch (start us, length us, event | category | flops | bytes accessed | tf_op | source)
XLA Modules:
  0.0 1027.6 jit_solution(12931380604742030447)
XLA Ops:
  7.2 3.6 collective-permute-start
  10.8 3.2 collective-permute-start.1
  39.2 1.7 fusion.186
  40.9 1.7 fusion.152
  42.6 2.0 fusion.156
  44.6 1.7 fusion.6
  52.7 1.7 fusion.22
  54.4 1.7 fusion.23
  56.1 1.7 fusion.184
  67.6 1.8 convolution_subtract_fusion.14
  79.4 2.1 fusion.13
  86.2 2.4 add_reduce_fusion.3
  92.0 1.9 fusion.11
  95.4 1.7 fusion.10
  105.3 1.9 fusion.42
  116.8 2.1 add_reduce_fusion.6
  122.3 1.7 fusion.19
  125.6 1.7 fusion.18
  130.4 1.7 convolution_add_fusion.18
  132.2 1.7 fusion.164
  142.2 1.8 fusion.117
  147.1 2.5 add_reduce_fusion
  153.0 1.7 fusion.3
  154.7 2.0 fusion.110
  156.7 1.7 fusion.2
  163.1 1.7 fusion.104
  166.5 1.7 fusion.9
  168.2 1.7 fusion.132
  170.0 1.7 fusion.8
  178.1 1.7 fusion.16
  179.8 1.8 fusion.158
  188.0 1.7 fusion
  191.3 1.8 convolution_subtract_fusion
  194.7 3.3 add_bitcast_fusion
  200.5 14.7 %dynamic_update_slice.9 = f32[4,512,384]{2,1,0:T(8,128)S(1)} dynamic-update-slice(f32[4,512,384]{2,1,0:T(8,128)S(1)} %broadcast_in_dim.2, f32[4,256,256]{2,1,0:T(8,128)} %pad_maximum_fusion, s32[]{:T(128)} %constant.21.clone.1, s32[]{:T(128)S(6)} %select_n.264, s32[]{:T(128)S(6)} %select_n.265) | dynamic-update-slice | bytes 2097156 | tf_op jit(solution)/shard_map/dynamic_update_slice | solution.py:120
  215.2 2.5 maximum_add_fusion
  217.6 14.2 %dynamic_update_slice.10 = f32[4,512,384]{2,1,0:T(8,128)S(1)} dynamic-update-slice(f32[4,512,384]{2,1,0:T(8,128)S(1)} %dynamic_update_slice.9, f32[4,256,256]{2,1,0:T(8,128)} %maximum_add_fusion, s32[]{:T(128)} %constant.21.clone.1, s32[]{:T(128)S(6)} %select_n.267, s32[]{:T(128)S(6)} %select_n.268) | dynamic-update-slice | bytes 2097156 | tf_op jit(solution)/shard_map/dynamic_update_slice | solution.py:120
  231.8 2.5 maximum_add_fusion.1
  234.4 14.2 %dynamic_update_slice.11 = f32[4,512,384]{2,1,0:T(8,128)S(1)} dynamic-update-slice(f32[4,512,384]{2,1,0:T(8,128)S(1)} %dynamic_update_slice.10, f32[4,256,256]{2,1,0:T(8,128)} %maximum_add_fusion.1, s32[]{:T(128)} %constant.21.clone.1, s32[]{:T(128)S(6)} %select_n.269, s32[]{:T(128)S(6)} %select_n.270) | dynamic-update-slice | bytes 2097156 | tf_op jit(solution)/shard_map/dynamic_update_slice | solution.py:120
  250.0 3.9 collective-permute-start.2
  253.9 2.9 collective-permute-start.3
  257.7 19.2 %collective-permute-done.2 = f32[4,512,128]{2,1,0:T(8,128)} collective-permute-done((f32[4,512,128]{2,1,0:T(8,128)}, f32[4,512,128]{2,1,0:T(8,128)}, u32[]{:S(2)}, u32[]{:S(2)}) %collective-permute-start.2) | collective-permute-done | bytes 1048608 | tf_op jit(solution)/shard_map/ppermute | solution.py:33
  276.9 4.6 collective-permute-done.3
  281.6 2.4 multiply_reduce_fusion.1
  284.0 114.2 %psum.21 = f32[]{:T(128)} all-reduce(f32[]{:T(128)} %multiply_reduce_fusion.1), channel_id=1, replica_groups=mesh['group'=4,'tile'=64] {'group','tile'}, use_global_device_ids=true, to_apply=%region_16.17 | all-reduce | flops 1 | bytes 8 | tf_op jit(solution)/shard_map/psum | solution.py:140
  398.9 3.0 slice_subtract_fusion
  402.0 614.2 %all-reduce.5.cloned.1.call-done = f32[1024,256]{1,0:T(8,128)} async-done(((f32[1024,256]{1,0:T(8,128)}), f32[1024,256]{1,0:T(8,128)}) %all-reduce.5.cloned.1.call-update) | async-done | bytes 1048592 | tf_op jit(solution)/shard_map/psum | solution.py:135
  1016.2 2.1 multiply_reduce_fusion
  (93 shorter events, 118.4 us)
Async XLA Ops:
  7.2 23.5 %copy-start.1 = (bf16[1,1,3,2,2,256,256]{6,5,4,3,2,1,0:T(8,128)(2,1)S(1)}, bf16[1,1,3,2,2,256,256]{6,5,4,3,2,1,0:T(8,128)(2,1)}, u32[]{:S(2)}) copy-start(bf16[1,1,3,2,2,256,256]{6,5,4,3,2,1,0:T(8,128)(2,1)} %param.8) | copy-start | bytes 4718596
  7.2 250.5 %all-reduce.3.cloned.1.call-start = ((), (), s32[]{:S(2)}) async-start(), calls=%async_computation | async-start | bytes 2097152 | tf_op jit(solution)/shard_map/psum | solution.py:135
  7.2 23.8 %collective-permute-start = (bf16[4,512,128]{2,1,0:T(8,128)(2,1)}, bf16[4,512,128]{2,1,0:T(8,128)(2,1)}, u32[]{:S(2)}, u32[]{:S(2)}) collective-permute-start(bf16[4,512,128]{2,1,0:T(8,128)(2,1)} %param.6), channel_id=1, source_target_pairs={{0,1},{1,2},{2,3},{3,4},{4,5},{5,6},{6,7},{7,8},{8,9},{9,10},{10,1... | collective-permute-start | bytes 1572872 | tf_op jit(solution)/shard_map/ppermute | solution.py:21
  10.8 20.1 %collective-permute-start.1 = (bf16[4,512,128]{2,1,0:T(8,128)(2,1)}, bf16[4,512,128]{2,1,0:T(8,128)(2,1)}, u32[]{:S(2)}, u32[]{:S(2)}) collective-permute-start(bf16[4,512,128]{2,1,0:T(8,128)(2,1)} %param.6), channel_id=1, source_target_pairs={{1,0},{2,1},{3,2},{4,3},{5,4},{6,5},{7,6},{8,7},{9,8},{10,9},{11,1... | collective-permute-start | bytes 1572872 | tf_op jit(solution)/shard_map/ppermute | solution.py:23
  25.8 5.2 copy-start.2
  32.4 1.7 copy-start
  69.4 4.8 copy-start.3
  199.2 817.0 %all-reduce.5.cloned.1.call-start = ((), (), s32[]{:S(2)}) async-start(), calls=%async_computation.1 | async-start | bytes 2097152 | tf_op jit(solution)/shard_map/psum | solution.py:135
  250.0 26.9 %collective-permute-start.2 = (f32[4,512,128]{2,1,0:T(8,128)}, f32[4,512,128]{2,1,0:T(8,128)}, u32[]{:S(2)}, u32[]{:S(2)}) collective-permute-start(f32[4,512,128]{2,1,0:T(8,128)} %get-tuple-element.30), channel_id=1, source_target_pairs={{1,0},{2,1},{3,2},{4,3},{5,4},{6,5},{7,6},{8,7},{9,8},{10,9},{11,1... | collective-permute-start | bytes 3145736 | tf_op jit(solution)/shard_map/ppermute | solution.py:33
  253.9 27.7 %collective-permute-start.3 = (f32[4,512,128]{2,1,0:T(8,128)}, f32[4,512,128]{2,1,0:T(8,128)}, u32[]{:S(2)}, u32[]{:S(2)}) collective-permute-start(f32[4,512,128]{2,1,0:T(8,128)} %get-tuple-element.31), channel_id=1, source_target_pairs={{0,1},{1,2},{2,3},{3,4},{4,5},{5,6},{6,7},{7,8},{8,9},{9,10},{10,1... | collective-permute-start | bytes 3145736 | tf_op jit(solution)/shard_map/ppermute | solution.py:33
Sparse Core Ops, SparseCore 0:
  199.3 58.2 all-reduce.2
  260.5 755.6 all-reduce.4
